TPU v7x, 32 devices: a whole 2x2x4 slice. The times are simulated.
32 devices in a mesh: section: 4 (over y, x), tile: 8 (over z, core).
Axes of the slice: x: 2, y: 2, z: 4, core: 2. Of those that a mesh axis runs over, the one named last changes fastest.
Arguments:
- queries: bfloat16 [4, 4096, 2560], P('section', 'tile'), may hold values from -60 to 60
- keys_values: bfloat16 [4, 2, 4096, 2560], P('section', None, 'tile'), may hold values from -6 to 6
- windows: int32 [16, 2], P('tile'), may hold values from 0 to 1
- gate_scales: float32 [4, 2560], P('section'), may hold values from 0.5 to 3
- stream_in: bfloat16 [4096, 2560], P('tile'), may hold values from -3 to 3
Outputs:
- streams: bfloat16 [4, 4096, 2560], P('section', 'tile')
All inputs are finite; a program needn't handle non-finite values.
Results may differ from a plain program's by a relative error of at most 0.005.
Values may be sent and summed in bfloat16 or wider, within the bound.
A program may use at most 128 MiB of HBM per device.

v0:
```python
import math

import jax
import jax.numpy as jnp
from jax import lax
from jax.sharding import PartitionSpec as P

HEAD_DIM = 128
TILE = 256
REACH = 1


def with_halo(block, sides, width):
    for axis, dim in sides:
        count = lax.axis_size(axis)
        forward = [(i, i + 1) for i in range(count - 1)]
        backward = [(target, source) for source, target in forward]
        low = lax.ppermute(
            lax.slice_in_dim(block, block.shape[dim] - width, None, axis=dim), axis, forward
        )
        high = lax.ppermute(lax.slice_in_dim(block, 0, width, axis=dim), axis, backward)
        block = jnp.concatenate([low, block, high], axis=dim)
    return block


def local(queries, keys_values, windows, gate_scales, stream_in):
    local_rows = queries.shape[1]
    width = queries.shape[2]
    local_tiles = local_rows // TILE
    head_count = width // HEAD_DIM
    extended = with_halo(keys_values, (("tile", 2),), REACH * TILE)
    first_tile = lax.axis_index("tile") * local_tiles
    total_tiles = local_tiles * lax.axis_size("tile")
    key_span = (2 * REACH + 1) * TILE
    score_scale = 1.0 / math.sqrt(HEAD_DIM)
    own_queries = queries[0]
    key_rows = extended[0, 0]
    value_rows = extended[0, 1]

    def one_tile(local_index):
        start = local_index * TILE
        query_block = lax.dynamic_slice_in_dim(own_queries, start, TILE, 0).reshape(
            TILE, head_count, HEAD_DIM
        )
        key_block = lax.dynamic_slice_in_dim(key_rows, start, key_span, 0).reshape(
            key_span, head_count, HEAD_DIM
        )
        value_block = lax.dynamic_slice_in_dim(value_rows, start, key_span, 0).reshape(
            key_span, head_count, HEAD_DIM
        )
        tile_global = first_tile + local_index
        key_tile = tile_global - REACH + jnp.arange(key_span, dtype=jnp.int32) // TILE
        reach_pair = lax.dynamic_slice_in_dim(windows, local_index, 1, 0)[0]
        allowed = (key_tile >= tile_global - reach_pair[0]) & (
            key_tile <= tile_global + reach_pair[1]
        )
        allowed = allowed & (key_tile >= 0) & (key_tile < total_tiles)
        scores = (
            jnp.einsum("qhd,khd->hqk", query_block, key_block, preferred_element_type=jnp.float32)
            * score_scale
        )
        scores = jnp.where(allowed[None, None, :], scores, -jnp.inf)
        row_max = jnp.max(scores, axis=-1, keepdims=True)
        exponent = jnp.exp(scores - row_max)
        weights = (exponent / jnp.sum(exponent, axis=-1, keepdims=True)).astype(jnp.bfloat16)
        attended = jnp.einsum(
            "hqk,khd->qhd", weights, value_block, preferred_element_type=jnp.float32
        )
        return attended.reshape(TILE, width)

    attended = lax.map(one_tile, jnp.arange(local_tiles, dtype=jnp.int32)).reshape(
        local_rows, width
    )
    shares = (gate_scales[0][None, :] * attended).astype(jnp.bfloat16)
    everyone = lax.all_gather(shares[None], "section", axis=0, tiled=True)
    position = lax.axis_index("section")
    selector = (jnp.arange(everyone.shape[0], dtype=jnp.int32) <= position).astype(jnp.bfloat16)
    summed = jnp.einsum("s,src->rc", selector, everyone, preferred_element_type=jnp.float32)
    streams = (stream_in.astype(jnp.float32) + summed).astype(jnp.bfloat16)
    return streams[None]


def solution(mesh):
    placed = (
        P("section", "tile", None),
        P("section", None, "tile", None),
        P("tile", None),
        P("section", None),
        P("tile", None),
    )
    return jax.shard_map(
        local, mesh=mesh, in_specs=placed, out_specs=P("section", "tile", None), check_vma=False
    )
```

profile of v0, /device:TPU:13, one launch (start us, length us, event | category | flops | bytes accessed | tf_op | source)
XLA Modules:
  0.0 301.8 jit_solution(5957503880521725503)
XLA Ops:
  6.5 4.5 %fusion.30 = (bf16[1,2,256,2560]{3,2,1,0:T(8,128)(2,1)S(1)}, bf16[1,2,256,2560]{3,2,1,0:T(8,128)(2,1)}) fusion(bf16[1,2,512,2560]{3,2,1,0:T(8,128)(2,1)} %param.8), kind=kLoop, calls=%fused_computation.49 | loop fusion | bytes 10485760 | tf_op jit(solution)/shard_map/slice | solution.py:21
  11.0 3.9 %collective-permute-start = (bf16[1,2,256,2560]{3,2,1,0:T(8,128)(2,1)}, bf16[1,2,256,2560]{3,2,1,0:T(8,128)(2,1)}, u32[]{:S(2)}, u32[]{:S(2)}) collective-permute-start(bf16[1,2,256,2560]{3,2,1,0:T(8,128)(2,1)} %get-tuple-element.173), channel_id=1, source_target_pairs={{0,1},{1,2},{2,3},{3,4},{4,5},{5,6},{6,7},{8,9},{9,10},{10,11},{11... | collective-permute-start | bytes 7864328 | tf_op jit(solution)/shard_map/ppermute | solution.py:18
  14.9 1.9 collective-permute-start.1
  16.9 4.4 %copy.14 = bf16[1,512,2560]{1,2,0:T(8,128)(2,1)} copy(bf16[1,512,2560]{2,1,0:T(8,128)(2,1)} %param.7) | data formatting | bytes 5242880 | tf_op args[0]
  21.3 0.6 reduce
  21.9 21.9 %collective-permute-done = bf16[1,2,256,2560]{3,2,1,0:T(8,128)(2,1)} collective-permute-done((bf16[1,2,256,2560]{3,2,1,0:T(8,128)(2,1)}, bf16[1,2,256,2560]{3,2,1,0:T(8,128)(2,1)}, u32[]{:S(2)}, u32[]{:S(2)}) %collective-permute-start) | collective-permute-done | bytes 2621472 | tf_op jit(solution)/shard_map/ppermute | solution.py:18
  43.8 3.4 %constant_dynamic-update-slice_fusion.3 = bf16[1,2,1024,2560]{3,2,1,0:T(8,128)(2,1)} fusion(bf16[1,2,256,2560]{3,2,1,0:T(8,128)(2,1)} %collective-permute-done), kind=kLoop, calls=%fused_computation.43 | loop fusion | bytes 5242880
  47.3 2.7 constant_dynamic-update-slice_fusion.2
  49.9 3.4 %constant_dynamic-update-slice_fusion.1 = bf16[1,2,1024,2560]{3,2,1,0:T(8,128)(2,1)} fusion(bf16[1,2,1024,2560]{3,2,1,0:T(8,128)(2,1)} %constant_dynamic-update-slice_fusion.2, bf16[1,2,256,2560]{3,2,1,0:T(8,128)(2,1)} %collective-permute-done.1), kind=kLoop, calls=%fused_computation.41 | loop fusion | bytes 5242880 | tf_op jit(solution)/shard_map/concatenate | solution.py:22
  53.3 8.7 %slice_bitcast_fusion = (bf16[1024,2560]{1,0:T(8,128)(2,1)}, bf16[1024,2560]{1,0:T(8,128)(2,1)}) fusion(bf16[1,2,1024,2560]{3,2,1,0:T(8,128)(2,1)} %constant_dynamic-update-slice_fusion.1), kind=kLoop, calls=%fused_computation.34 | loop fusion | bytes 20971520 | tf_op jit(solution)/shard_map/squeeze | solution.py:37
  62.0 99.3 %while.13 = (s32[]{:T(128)}, f32[2,256,2560]{2,1,0:T(8,128)}, s32[2]{0:T(128)S(1)}, bf16[1024,2560]{1,0:T(8,128)(2,1)}, s32[]{:T(128)}, /*index=5*/s32[2,2]{1,0:...) while((s32[]{:T(128)}, f32[2,256,2560]{2,1,0:T(8,128)}, ...), condition=%wide.region_3.4_spmd, body=%wide.region_0.3_spmd.sunk | while | flops 2036871936 | bytes 87861608 | solution.py:71
  67.8 6.9 %constant_dynamic-slice_fusion.7 = (bf16[768,2560]{1,0:T(8,128)(2,1)}, bf16[768,2560]{1,0:T(8,128)(2,1)}) fusion(bf16[1024,2560]{1,0:T(8,128)(2,1)} %get-tuple-element.272, s32[]{:T(128)S(6)} %select_n.83, bf16[1024,2560]{1,0:T(8,128)(2,1)} %get-tuple-element.268), kind=kLoop, calls=%fused_computation.26.clone.1 | loop fusion | bytes 15728644 | tf_op jit(solution)/shard_map/while/body/eval_jaxpr/dynamic_slice | solution.py:45
  74.7 6.3 %copy.35 = bf16[768,2560]{0,1:T(8,128)(2,1)} copy(bf16[768,2560]{1,0:T(8,128)(2,1)} %get-tuple-element.232) | data formatting | bytes 7864320 | tf_op jit(solution)/shard_map/while/body/eval_jaxpr/dynamic_slice | solution.py:45
  81.0 1.4 constant_dynamic-slice_fusion.9
  82.4 10.1 %fusion.48 = (f32[20,256]{1,0:T(8,128)S(1)}, f32[20,256,768]{2,1,0:T(8,128)}) fusion(pred[768]{0:T(1024)(128)(4,1)S(1)} %fusion.47, bf16[256,20,128]{0,2,1:T(8,128)(2,1)S(1)} %bitcast.58, bf16[768,20,128]{0,2,1:T(8,128)(2,1)} %bitcast.55), kind=kOutput, calls=%fused_computation.48.clone.1 | convolution fusion | flops 1022362368 | bytes 20992768 | tf_op jit(solution)/shard_map/while/body/eval_jaxpr/sub | solution.py:64
  92.5 6.3 %copy.34 = bf16[768,2560]{0,1:T(8,128)(2,1)} copy(bf16[768,2560]{1,0:T(8,128)(2,1)} %get-tuple-element.229) | data formatting | bytes 7864320 | tf_op jit(solution)/shard_map/while/body/eval_jaxpr/dynamic_slice | solution.py:48
  98.8 9.1 %fusion.49 = f32[20,128,256]{2,1,0:T(8,128)} fusion(bf16[768,20,128]{0,2,1:T(8,128)(2,1)} %bitcast.56, f32[20,256,768]{2,1,0:T(8,128)} %get-tuple-element.233, f32[20,256]{1,0:T(8,128)S(1)} %get-tuple-element.234), kind=kOutput, calls=%fused_computation.7.clone.1 | convolution fusion | flops 1014497280 | bytes 22302720 | tf_op jit(solution)/shard_map/while/body/eval_jaxpr/hqk,khd->qhd/dot_general | solution.py:66
  107.8 2.1 copy.36
  110.0 1.6 constant_dynamic-update-slice_fusion.5
  114.2 0.6 fusion.46
  117.4 6.9 %constant_dynamic-slice_fusion.7 = (bf16[768,2560]{1,0:T(8,128)(2,1)}, bf16[768,2560]{1,0:T(8,128)(2,1)}) fusion(bf16[1024,2560]{1,0:T(8,128)(2,1)} %get-tuple-element.272, s32[]{:T(128)S(6)} %select_n.83, bf16[1024,2560]{1,0:T(8,128)(2,1)} %get-tuple-element.268), kind=kLoop, calls=%fused_computation.26.clone.1 | loop fusion | bytes 15728644 | tf_op jit(solution)/shard_map/while/body/eval_jaxpr/dynamic_slice | solution.py:45
  124.3 6.3 %copy.35 = bf16[768,2560]{0,1:T(8,128)(2,1)} copy(bf16[768,2560]{1,0:T(8,128)(2,1)} %get-tuple-element.232) | data formatting | bytes 7864320 | tf_op jit(solution)/shard_map/while/body/eval_jaxpr/dynamic_slice | solution.py:45
  130.6 1.4 constant_dynamic-slice_fusion.9
  132.0 10.1 %fusion.48 = (f32[20,256]{1,0:T(8,128)S(1)}, f32[20,256,768]{2,1,0:T(8,128)}) fusion(pred[768]{0:T(1024)(128)(4,1)S(1)} %fusion.47, bf16[256,20,128]{0,2,1:T(8,128)(2,1)S(1)} %bitcast.58, bf16[768,20,128]{0,2,1:T(8,128)(2,1)} %bitcast.55), kind=kOutput, calls=%fused_computation.48.clone.1 | convolution fusion | flops 1022362368 | bytes 20992768 | tf_op jit(solution)/shard_map/while/body/eval_jaxpr/sub | solution.py:64
  142.1 6.3 %copy.34 = bf16[768,2560]{0,1:T(8,128)(2,1)} copy(bf16[768,2560]{1,0:T(8,128)(2,1)} %get-tuple-element.229) | data formatting | bytes 7864320 | tf_op jit(solution)/shard_map/while/body/eval_jaxpr/dynamic_slice | solution.py:48
  148.4 9.1 %fusion.49 = f32[20,128,256]{2,1,0:T(8,128)} fusion(bf16[768,20,128]{0,2,1:T(8,128)(2,1)} %bitcast.56, f32[20,256,768]{2,1,0:T(8,128)} %get-tuple-element.233, f32[20,256]{1,0:T(8,128)S(1)} %get-tuple-element.234), kind=kOutput, calls=%fused_computation.7.clone.1 | convolution fusion | flops 1014497280 | bytes 22302720 | tf_op jit(solution)/shard_map/while/body/eval_jaxpr/hqk,khd->qhd/dot_general | solution.py:66
  157.4 2.1 copy.36
  159.6 1.7 constant_dynamic-update-slice_fusion.5
  161.3 4.5 %fusion.24 = bf16[1,512,2560]{2,1,0:T(8,128)(2,1)} fusion(f32[2560]{0:T(1024)S(1)} %copy-done.2, f32[1,512,2560]{2,1,0:T(8,128)} %bitcast.60), kind=kLoop, calls=%fused_computation.39 | loop fusion | flops 2621440 | bytes 7874560 | tf_op jit(solution)/shard_map/convert_element_type | solution.py:74
  165.8 106.9 %all-gather.2.cloned.1.call-done = bf16[4,512,2560]{2,1,0:T(8,128)(2,1)} async-done(((bf16[1,512,2560]{2,1,0:T(8,128)(2,1)}), bf16[4,512,2560]{2,1,0:T(8,128)(2,1)}) %all-gather.2.cloned.1.call-update) | async-done | bytes 10485776 | tf_op jit(solution)/shard_map/all_gather | solution.py:75
  272.8 19.8 %fusion.21 = f32[1,512,2560]{2,0,1:T(1,128)S(1)} fusion(bf16[4,512,2560]{2,1,0:T(8,128)(2,1)} %all-gather.2.cloned.1.call-done, s32[]{:T(128)S(6)} %axis_index.23), kind=kOutput, calls=%fused_computation.32 | convolution fusion | flops 10485764 | bytes 15728644 | tf_op jit(solution)/shard_map/s,src->rc/dot_general | solution.py:78
  292.6 2.4 fusion.25
  (22 shorter events, 1.9 us)
Async XLA Ops:
  6.5 266.2 %all-gather.2.cloned.1.call-start = ((), (), s32[]{:S(2)}) async-start(), calls=%async_computation | async-start | bytes 13107200 | tf_op jit(solution)/shard_map/all_gather | solution.py:75
  11.0 10.3 %copy-start.3 = (f32[1,2560]{1,0:T(1,128)S(1)}, f32[1,2560]{1,0:T(1,128)}, u32[]{:S(2)}) copy-start(f32[1,2560]{1,0:T(1,128)} %param.10) | copy-start | bytes 30724
  11.0 32.8 %collective-permute-start = (bf16[1,2,256,2560]{3,2,1,0:T(8,128)(2,1)}, bf16[1,2,256,2560]{3,2,1,0:T(8,128)(2,1)}, u32[]{:S(2)}, u32[]{:S(2)}) collective-permute-start(bf16[1,2,256,2560]{3,2,1,0:T(8,128)(2,1)} %get-tuple-element.173), channel_id=1, source_target_pairs={{0,1},{1,2},{2,3},{3,4},{4,5},{5,6},{6,7},{8,9},{9,10},{10,11},{11... | collective-permute-start | bytes 7864328 | tf_op jit(solution)/shard_map/ppermute | solution.py:18
  14.9 35.0 %collective-permute-start.1 = (bf16[1,2,256,2560]{3,2,1,0:T(8,128)(2,1)S(1)}, bf16[1,2,256,2560]{3,2,1,0:T(8,128)(2,1)}, u32[]{:S(2)}, u32[]{:S(2)}) collective-permute-start(bf16[1,2,256,2560]{3,2,1,0:T(8,128)(2,1)S(1)} %get-tuple-element.172), channel_id=1, source_target_pairs={{1,0},{2,1},{3,2},{4,3},{5,4},{6,5},{7,6},{9,8},{10,9},{11,10},{12... | collective-permute-start | bytes 7864328 | tf_op jit(solution)/shard_map/ppermute | solution.py:21
  21.9 25.3 %copy-start = (bf16[1,2,512,2560]{3,2,1,0:T(8,128)(2,1)S(1)}, bf16[1,2,512,2560]{3,2,1,0:T(8,128)(2,1)}, u32[]{:S(2)}) copy-start(bf16[1,2,512,2560]{3,2,1,0:T(8,128)(2,1)} %param.8) | copy-start | bytes 15728644
  53.3 8.7 %copy-start.4 = (s32[2,2]{1,0:T(2,128)S(1)}, s32[2,2]{1,0:T(2,128)}, u32[]{:S(2)}) copy-start(s32[2,2]{1,0:T(2,128)} %param.9) | copy-start | bytes 52
  62.0 99.3 %copy-start.2 = (f32[2560]{0:T(1024)S(1)}, f32[2560]{0:T(1024)}, u32[]{:S(2)}) copy-start(f32[2560]{0:T(1024)} %reduce) | copy-start | bytes 30724
  165.8 126.7 %copy-start.1 = (bf16[512,2560]{1,0:T(8,128)(2,1)S(1)}, bf16[512,2560]{1,0:T(8,128)(2,1)}, u32[]{:S(2)}) copy-start(bf16[512,2560]{1,0:T(8,128)(2,1)} %param.11) | copy-start | bytes 7864324
Sparse Core Ops, SparseCore 0:
  165.9 106.7 all-gather.1
where the time goes:
time: 305 us; the launch traced here: 302 us
  waiting for transfers between devices  129 us (42%)
  local copies, waits for them, and re-layouts  78.9 us (26%)
  matrix products  58.1 us (19%)
  between operations  13.5 us (4%)
  loops' own time  9.13 us (3%)
  other arithmetic  7.58 us (2%)
  starting transfers between devices  5.81 us (2%)
    all_gather x1, waiting for transfers between devices, local(): everyone = lax.all_gather(shares[None], 'section', axis=0, tiled=True)  107 us
    dynamic_slice x4, local copies, waits for them, and re-layouts, one_tile(): lax.dynamic_slice_in_dim(key_rows, start, key_span, 0)  26.4 us
    ppermute x1, waiting for transfers between devices, with_halo(): lax.ppermute(lax.slice_in_dim(block, block.shape[dim] - width, None, axis...  21.9 us
    sub x2, matrix products, one_tile(): exponent = jnp.exp(scores - row_max)  20.2 us
    dot_general x1, matrix products, local(): jnp.einsum('s,src->rc', selector, everyone, preferred_element_type=jnp.fl...  19.8 us
    dot_general x2, matrix products, one_tile(): jnp.einsum('hqk,khd->qhd', weights, value_block, preferred_element_type=j...  18.1 us
    dynamic_slice x2, local copies, waits for them, and re-layouts, one_tile(): lax.dynamic_slice_in_dim(value_rows, start, key_span, 0)  12.5 us
    unnamed x13, local copies, waits for them, and re-layouts  10.5 us
  transfers between devices with their start and end apart: 3, of which 2 were waited for; matrix products, arithmetic and copies ran while one was open for 4% of the time, Pallas kernels for 0%

commit v1 on v0

v1 whole, which is shorter than its diff:
```python
import functools
import math

import jax
import jax.numpy as jnp
from jax import lax
from jax.experimental import pallas as pl
from jax.experimental.pallas import tpu as pltpu
from jax.sharding import PartitionSpec as P

HEAD_DIM = 128
TILE = 256
REACH = 1
HALO = REACH * TILE
LAG = 2
AHEAD = 3
FAR = 1e30
VMEM_BYTES = 56 * 1024 * 1024


def kernel(
    sections, tiles_axis,
    windows, queries, keys_values, gates, stream_in, out,
    q_buf, kv_buf, low, high, in_buf, share, recv, fwd, out_buf,
    q_sem, kv_sem, in_sem, out_sem, halo_send, halo_recv, sec_send, sec_recv,
):
    heads, rows = q_buf.shape[0], q_buf.shape[1]
    local_tiles = rows // TILE
    stages = sections.bit_length() - 1
    section = lax.axis_index("section")
    place = lax.axis_index("tile")
    has_left = place > 0
    has_right = place < tiles_axis - 1

    def partner(stage):
        d = 1 << stage
        return section + d - 2 * d * ((section // d) % 2)

    def sends(who, stage):
        return who // (1 << stage) < sections // (1 << stage) - 1

    def receives(stage):
        return sends(partner(stage), stage)

    def above(stage):
        return (section // (1 << stage)) % 2 == 1

    def columns(head):
        return pl.ds(pl.multiple_of(head * HEAD_DIM, HEAD_DIM), HEAD_DIM)

    def loads(head):
        cols = columns(head)
        return (
            pltpu.make_async_copy(
                keys_values.at[0, :, :, cols], kv_buf.at[head], kv_sem.at[head]
            ),
            pltpu.make_async_copy(queries.at[0, :, cols], q_buf.at[head], q_sem.at[head]),
            pltpu.make_async_copy(stream_in.at[:, cols], in_buf.at[head], in_sem.at[head]),
        )

    def to_right(head):
        return pltpu.make_async_remote_copy(
            src_ref=keys_values.at[0, :, pl.ds(rows - HALO, HALO), columns(head)],
            dst_ref=low.at[head],
            send_sem=halo_send.at[0, head],
            recv_sem=halo_recv.at[0, head],
            device_id={"tile": place + 1},
            device_id_type=pl.DeviceIdType.MESH,
        )

    def to_left(head):
        return pltpu.make_async_remote_copy(
            src_ref=keys_values.at[0, :, pl.ds(0, HALO), columns(head)],
            dst_ref=high.at[head],
            send_sem=halo_send.at[1, head],
            recv_sem=halo_recv.at[1, head],
            device_id={"tile": place - 1},
            device_id_type=pl.DeviceIdType.MESH,
        )

    def to_partner(stage, head):
        source = share.at[head] if stage == 0 else fwd.at[stage - 1, head]
        return pltpu.make_async_remote_copy(
            src_ref=source,
            dst_ref=recv.at[stage, head],
            send_sem=sec_send.at[stage, head],
            recv_sem=sec_recv.at[stage, head],
            device_id={"section": partner(stage)},
            device_id_type=pl.DeviceIdType.MESH,
        )

    def load(head):
        for copy in loads(head):
            copy.start()

    def send_halo(head):
        @pl.when(has_right)
        def _():
            to_right(head).start()

        @pl.when(has_left)
        def _():
            to_left(head).start()

    barrier = pltpu.get_barrier_semaphore()

    @pl.when(has_right)
    def _():
        pl.semaphore_signal(
            barrier, inc=1, device_id={"tile": place + 1}, device_id_type=pl.DeviceIdType.MESH
        )

    @pl.when(has_left)
    def _():
        pl.semaphore_signal(
            barrier, inc=1, device_id={"tile": place - 1}, device_id_type=pl.DeviceIdType.MESH
        )

    for stage in range(stages):
        pl.semaphore_signal(
            barrier, inc=1, device_id={"section": partner(stage)},
            device_id_type=pl.DeviceIdType.MESH,
        )
    ahead = min(AHEAD, heads)
    for head in range(ahead):
        load(head)

    def clear(ref):
        def one(head, carry):
            ref[head] = jnp.zeros(ref.shape[1:], ref.dtype)
            return carry

        lax.fori_loop(0, heads, one, 0)

    pl.when(jnp.logical_not(has_left))(lambda: clear(low))
    pl.when(jnp.logical_not(has_right))(lambda: clear(high))

    pl.semaphore_wait(barrier, stages + has_left.astype(jnp.int32) + has_right.astype(jnp.int32))
    for head in range(ahead):
        send_halo(head)

    factor = math.log2(math.e) / math.sqrt(HEAD_DIM)

    def attend(head):
        gate = gates[:, columns(head)]

        def block(index, which):
            if index < 0:
                return low[head, which, pl.ds((index + REACH) * TILE, TILE), :]
            if index >= local_tiles:
                return high[head, which, pl.ds((index - local_tiles) * TILE, TILE), :]
            return kv_buf[head, which, pl.ds(index * TILE, TILE), :]

        for tile in reversed(range(local_tiles)):
            span = pl.ds(tile * TILE, TILE)
            query = q_buf[head, span, :]
            offsets = range(-REACH, REACH + 1)
            at = place * local_tiles + tile
            allowed, scores, tops = [], [], []
            for offset in offsets:
                score = lax.dot_general(
                    query, block(tile + offset, 0), (((1,), (1,)), ((), ())),
                    preferred_element_type=jnp.float32,
                )
                top = jnp.max(score, axis=-1, keepdims=True)
                if offset < 0:
                    ok = (windows[tile, 0] >= -offset) & (at + offset >= 0)
                elif offset > 0:
                    ok = (windows[tile, 1] >= offset) & (at + offset < tiles_axis * local_tiles)
                else:
                    ok = None
                allowed.append(ok)
                scores.append(score)
                tops.append(top if ok is None else jnp.where(ok, top, -FAR))
            row_max = functools.reduce(jnp.maximum, tops)
            total = jnp.zeros((TILE, 1), jnp.float32)
            attended = jnp.zeros((TILE, HEAD_DIM), jnp.float32)
            for offset, ok, score in zip(offsets, allowed, scores):
                shift = row_max if ok is None else jnp.where(ok, row_max, FAR)
                weight = jnp.exp2((score - shift) * factor)
                total = total + jnp.sum(weight, axis=-1, keepdims=True)
                attended = attended + jnp.dot(
                    weight.astype(jnp.bfloat16), block(tile + offset, 1),
                    preferred_element_type=jnp.float32,
                )
            share[head, span, :] = (gate * (attended / total)).astype(jnp.bfloat16)

    def compute(head):
        @pl.when(head + ahead < heads)
        def _():
            load(head + ahead)
            send_halo(head + ahead)

        for copy in loads(head):
            copy.wait()

        @pl.when(has_right)
        def _():
            to_left(head).wait_recv()

        @pl.when(has_left)
        def _():
            to_right(head).wait_recv()

        attend(head)
        if stages > 0:
            @pl.when(sends(section, 0))
            def _():
                to_partner(0, head).start()

    def combine(stage, head):
        @pl.when(receives(stage))
        def _():
            to_partner(stage, head).wait_recv()

        if stage < stages - 1:
            @pl.when(sends(section, stage + 1))
            def _():
                held = share[head] if stage == 0 else fwd[stage - 1, head]
                both = held.astype(jnp.float32) + recv[stage, head].astype(jnp.float32)
                fwd[stage, head] = both.astype(jnp.bfloat16)
                to_partner(stage + 1, head).start()

    def finish(head):
        out_buf[head] = in_buf[head].astype(jnp.float32) + share[head].astype(jnp.float32)
        for stage in range(stages):
            @pl.when(above(stage))
            def _():
                out_buf[head] += recv[stage, head].astype(jnp.float32)
        in_buf[head] = out_buf[head].astype(jnp.bfloat16)
        result(head).start()

    def result(head):
        return pltpu.make_async_copy(
            in_buf.at[head], out.at[0, :, columns(head)], out_sem.at[head]
        )

    def step(count, carry):
        pl.when(count < heads)(lambda: compute(count))
        for stage in range(stages):
            head = count - (stage + 1) * LAG

            @pl.when((head >= 0) & (head < heads))
            def _():
                combine(stage, head)

        head = count - stages * LAG

        @pl.when((head >= 0) & (head < heads))
        def _():
            finish(head)

        return carry

    lax.fori_loop(0, heads + stages * LAG, step, 0)

    def drain(head, carry):
        result(head).wait()

        @pl.when(has_right)
        def _():
            to_right(head).wait_send()

        @pl.when(has_left)
        def _():
            to_left(head).wait_send()

        for stage in range(stages):
            @pl.when(sends(section, stage))
            def _():
                to_partner(stage, head).wait_send()

        return carry

    lax.fori_loop(0, heads, drain, 0)


def local(sections, tiles_axis, queries, keys_values, windows, gate_scales, stream_in):
    rows, width = queries.shape[1], queries.shape[2]
    heads = width // HEAD_DIM
    stages = sections.bit_length() - 1
    assert sections == 1 << stages
    half = (heads, rows, HEAD_DIM)
    anywhere = pl.BlockSpec(memory_space=pl.ANY)
    dma = pltpu.SemaphoreType.DMA
    return pl.pallas_call(
        functools.partial(kernel, sections, tiles_axis),
        out_shape=jax.ShapeDtypeStruct((1, rows, width), jnp.bfloat16),
        in_specs=[
            pl.BlockSpec(memory_space=pltpu.SMEM),
            anywhere,
            anywhere,
            pl.BlockSpec(memory_space=pltpu.VMEM),
            anywhere,
        ],
        out_specs=anywhere,
        scratch_shapes=[
            pltpu.VMEM(half, jnp.bfloat16),
            pltpu.VMEM((heads, 2, rows, HEAD_DIM), jnp.bfloat16),
            pltpu.VMEM((heads, 2, HALO, HEAD_DIM), jnp.bfloat16),
            pltpu.VMEM((heads, 2, HALO, HEAD_DIM), jnp.bfloat16),
            pltpu.VMEM(half, jnp.bfloat16),
            pltpu.VMEM(half, jnp.bfloat16),
            pltpu.VMEM((max(stages, 1),) + half, jnp.bfloat16),
            pltpu.VMEM((max(stages - 1, 1),) + half, jnp.bfloat16),
            pltpu.VMEM(half, jnp.float32),
            dma((heads,)),
            dma((heads,)),
            dma((heads,)),
            dma((heads,)),
            dma((2, heads)),
            dma((2, heads)),
            dma((max(stages, 1), heads)),
            dma((max(stages, 1), heads)),
        ],
        compiler_params=pltpu.CompilerParams(
            collective_id=0, has_side_effects=True, vmem_limit_bytes=VMEM_BYTES
        ),
    )(windows, queries, keys_values, gate_scales, stream_in)


def solution(mesh):
    placed = (
        P("section", "tile", None),
        P("section", None, "tile", None),
        P("tile", None),
        P("section", None),
        P("tile", None),
    )
    return jax.shard_map(
        functools.partial(local, mesh.shape["section"], mesh.shape["tile"]),
        mesh=mesh, in_specs=placed, out_specs=P("section", "tile", None), check_vma=False,
    )
```

time: 305 us -> 76.2 us (0.25)
  waiting for transfers between devices: 129 us -> 0 us
  local copies, waits for them, and re-layouts: 78.9 us -> 3.4 us
  Pallas kernels: 0 us -> 72.5 us
  matrix products: 58.1 us -> 0 us
  between operations: 13.5 us -> 0.01 us
  loops' own time: 9.13 us -> 0 us
  other arithmetic: 7.58 us -> 0 us
  starting transfers between devices: 5.81 us -> 0 us
    all_gather x1 -> x0, waiting for transfers between devices: 107 us -> none  [local(): everyone = lax.all_gather(shares[None], 'section', axis=0, tiled=True)]
    pallas_call x0 -> x1, Pallas kernels: none -> 72.5 us  [local(): pl.pallas_call(functools.partial(kernel, sections, tiles_axis), out_shape...]
    dynamic_slice x12 -> x0, local copies, waits for them, and re-layouts: 42.9 us -> none  [the longest x4 26.4 us: one_tile(): lax.dynamic_slice_in_dim(key_rows, start, key_span, 0)]
    dot_general x3 -> x0, matrix products: 37.9 us -> none  [the longest x1 19.8 us: local(): jnp.einsum('s,src->rc', selector, everyone, preferred_element_type=jnp.fl...]
    ppermute x2 -> x0, waiting for transfers between devices: 21.9 us -> none  [the longest x1 21.9 us: with_halo(): lax.ppermute(lax.slice_in_dim(block, block.shape[dim] - width, None, axis...]
    sub x2 -> x0, matrix products: 20.2 us -> none  [one_tile(): exponent = jnp.exp(scores - row_max)]
    another operation x1 -> x0, loops' own time: 9.13 us -> none  [local(): lax.map(one_tile, jnp.arange(local_tiles, dtype=jnp.int32))]
    squeeze x1 -> x0, local copies, waits for them, and re-layouts: 8.67 us -> none  [local(): key_rows = extended[0, 0]]
  transfers between devices with their start and end apart: 3 -> 0, of which waited for: 2 -> 0; matrix products, arithmetic and copies ran while one was open for 4% -> 0% of each run, Pallas kernels for 0% -> 0%
where the time goes in v1:
time: 76.2 us; the launch traced here: 75.9 us
  Pallas kernels  72.5 us (95%)
  local copies, waits for them, and re-layouts  3.4 us (4%)
    pallas_call x1, Pallas kernels, local(): pl.pallas_call(functools.partial(kernel, sections, tiles_axis), out_shape...  72.5 us
    unnamed x1, local copies, waits for them, and re-layouts  3.4 us

profile of v1, /device:TPU:13, one launch (start us, length us, event | category | flops | bytes accessed | tf_op | source)
XLA Modules:
  0.0 75.9 jit_solution(11163636377134732797)
XLA Ops:
  0.0 72.5 %shard_map.55 = bf16[1,512,2560]{2,1,0:T(8,128)(2,1)} custom-call(s32[2,2]{1,0:T(2,128)} %windows.1, bf16[1,512,2560]{2,1,0:T(8,128)(2,1)} %queries.1, bf16[1,2,512,2560]{3,2,1,0:T(8,128)(2,1)} %keys_values.1, f32[1,2560]{1,0:T(1,128)} %gates.1, bf16[512,2560]{1,0:T(8,128)(2,1)} %stream_in.1), custom_call_target="tpu_custom_call" | custom-call | tf_op jit(solution)/shard_map/pallas_call | solution.py:286
  72.5 3.4 %copy.7 = bf16[1,512,2560]{2,1,0:T(8,128)(2,1)} copy(bf16[1,512,2560]{2,1,0:T(8,128)(2,1)} %shard_map.55) | data formatting | bytes 5242880

commit v2 on v1

v2 whole, which is shorter than its diff:
```python
import functools
import math

import jax
import jax.numpy as jnp
from jax import lax
from jax.experimental import pallas as pl
from jax.experimental.pallas import tpu as pltpu
from jax.sharding import PartitionSpec as P

HEAD_DIM = 128
TILE = 256
REACH = 1
HALO = REACH * TILE
LAG = 3
AHEAD = 3
FAR = 1e30
VMEM_BYTES = 50 * 1024 * 1024


def kernel(
    sections, tiles_axis,
    windows, queries, keys_values, gates, stream_in, out,
    q_buf, kv_buf, low, high, in_buf, share, recv, fwd, out_buf,
    q_sem, kv_sem, in_sem, halo_send, halo_recv, sec_send, sec_recv,
):
    heads, rows = q_buf.shape[0], q_buf.shape[1]
    local_tiles = rows // TILE
    units = heads * local_tiles
    stages = sections.bit_length() - 1
    section = lax.axis_index("section")
    place = lax.axis_index("tile")
    has_left = place > 0
    has_right = place < tiles_axis - 1

    def partner(stage):
        d = 1 << stage
        return section + d - 2 * d * ((section // d) % 2)

    def sends(who, stage):
        return who // (1 << stage) < sections // (1 << stage) - 1

    def receives(stage):
        return sends(partner(stage), stage)

    def above(stage):
        return (section // (1 << stage)) % 2 == 1

    def columns(head):
        return pl.ds(pl.multiple_of(head * HEAD_DIM, HEAD_DIM), HEAD_DIM)

    def loads(head):
        cols = columns(head)
        return (
            pltpu.make_async_copy(
                keys_values.at[0, :, :, cols], kv_buf.at[head], kv_sem.at[head]
            ),
            pltpu.make_async_copy(queries.at[0, :, cols], q_buf.at[head], q_sem.at[head]),
            pltpu.make_async_copy(stream_in.at[:, cols], in_buf.at[head], in_sem.at[head]),
        )

    def to_right(head):
        return pltpu.make_async_remote_copy(
            src_ref=keys_values.at[0, :, pl.ds(rows - HALO, HALO), columns(head)],
            dst_ref=low.at[head],
            send_sem=halo_send.at[0, head],
            recv_sem=halo_recv.at[0, head],
            device_id={"tile": place + 1},
            device_id_type=pl.DeviceIdType.MESH,
        )

    def to_left(head):
        return pltpu.make_async_remote_copy(
            src_ref=keys_values.at[0, :, pl.ds(0, HALO), columns(head)],
            dst_ref=high.at[head],
            send_sem=halo_send.at[1, head],
            recv_sem=halo_recv.at[1, head],
            device_id={"tile": place - 1},
            device_id_type=pl.DeviceIdType.MESH,
        )

    def where(unit):
        head, order = unit // local_tiles, unit % local_tiles
        inner = place % 2
        tile = order * inner + (local_tiles - 1 - order) * (1 - inner)
        return head, tile, pl.ds(pl.multiple_of(tile * TILE, TILE), TILE)

    def to_partner(stage, unit):
        head, tile, span = where(unit)
        source = share.at[head, span] if stage == 0 else fwd.at[stage - 1, head, span]
        return pltpu.make_async_remote_copy(
            src_ref=source,
            dst_ref=recv.at[stage, head, span],
            send_sem=sec_send.at[stage, unit],
            recv_sem=sec_recv.at[stage, unit],
            device_id={"section": partner(stage)},
            device_id_type=pl.DeviceIdType.MESH,
        )

    def load(head):
        for copy in loads(head):
            copy.start()

    def send_halo(head):
        @pl.when(has_right)
        def _():
            to_right(head).start()

        @pl.when(has_left)
        def _():
            to_left(head).start()

    barrier = pltpu.get_barrier_semaphore()

    @pl.when(has_right)
    def _():
        pl.semaphore_signal(
            barrier, inc=1, device_id={"tile": place + 1}, device_id_type=pl.DeviceIdType.MESH
        )

    @pl.when(has_left)
    def _():
        pl.semaphore_signal(
            barrier, inc=1, device_id={"tile": place - 1}, device_id_type=pl.DeviceIdType.MESH
        )

    for stage in range(stages):
        pl.semaphore_signal(
            barrier, inc=1, device_id={"section": partner(stage)},
            device_id_type=pl.DeviceIdType.MESH,
        )
    ahead = min(AHEAD, heads)
    for head in range(ahead):
        load(head)

    def clear(ref):
        def one(head, carry):
            ref[head] = jnp.zeros(ref.shape[1:], ref.dtype)
            return carry

        lax.fori_loop(0, heads, one, 0)

    pl.when(jnp.logical_not(has_left))(lambda: clear(low))
    pl.when(jnp.logical_not(has_right))(lambda: clear(high))

    pl.semaphore_wait(barrier, stages + has_left.astype(jnp.int32) + has_right.astype(jnp.int32))
    for head in range(ahead):
        send_halo(head)

    factor = math.log2(math.e) / math.sqrt(HEAD_DIM)

    def attend(head, tile):
        gate = gates[:, columns(head)]

        def block(index, which):
            if index < 0:
                return low[head, which, pl.ds((index + REACH) * TILE, TILE), :]
            if index >= local_tiles:
                return high[head, which, pl.ds((index - local_tiles) * TILE, TILE), :]
            return kv_buf[head, which, pl.ds(index * TILE, TILE), :]

        span = pl.ds(tile * TILE, TILE)
        query = q_buf[head, span, :]
        offsets = range(-REACH, REACH + 1)
        at = place * local_tiles + tile
        allowed, scores, tops = [], [], []
        for offset in offsets:
            score = lax.dot_general(
                query, block(tile + offset, 0), (((1,), (1,)), ((), ())),
                preferred_element_type=jnp.float32,
            )
            top = jnp.max(score, axis=-1, keepdims=True)
            if offset < 0:
                ok = (windows[tile, 0] >= -offset) & (at + offset >= 0)
            elif offset > 0:
                ok = (windows[tile, 1] >= offset) & (at + offset < tiles_axis * local_tiles)
            else:
                ok = None
            allowed.append(ok)
            scores.append(score)
            tops.append(top if ok is None else jnp.where(ok, top, -FAR))
        row_max = functools.reduce(jnp.maximum, tops)
        total = jnp.zeros((TILE, 1), jnp.float32)
        attended = jnp.zeros((TILE, HEAD_DIM), jnp.float32)
        for offset, ok, score in zip(offsets, allowed, scores):
            shift = row_max if ok is None else jnp.where(ok, row_max, FAR)
            weight = jnp.exp2((score - shift) * factor)
            total = total + jnp.sum(weight, axis=-1, keepdims=True)
            attended = attended + jnp.dot(
                weight.astype(jnp.bfloat16), block(tile + offset, 1),
                preferred_element_type=jnp.float32,
            )
        share[head, span, :] = (gate * (attended / total)).astype(jnp.bfloat16)

    def compute(unit):
        head, tile, _ = where(unit)

        @pl.when(unit % local_tiles == 0)
        def _():
            @pl.when(head + ahead < heads)
            def _():
                load(head + ahead)
                send_halo(head + ahead)

            for copy in loads(head):
                copy.wait()

        for at in range(local_tiles):
            @pl.when(tile == at)
            def _():
                if at == 0:
                    @pl.when(has_left)
                    def _():
                        to_right(head).wait_recv()

                if at == local_tiles - 1:
                    @pl.when(has_right)
                    def _():
                        to_left(head).wait_recv()

                attend(head, at)

        if stages > 0:
            @pl.when(sends(section, 0))
            def _():
                to_partner(0, unit).start()

    def combine(stage, unit):
        @pl.when(receives(stage))
        def _():
            to_partner(stage, unit).wait_recv()

        if stage < stages - 1:
            @pl.when(sends(section, stage + 1))
            def _():
                head, tile, span = where(unit)
                held = share[head, span] if stage == 0 else fwd[stage - 1, head, span]
                both = held.astype(jnp.float32) + recv[stage, head, span].astype(jnp.float32)
                fwd[stage, head, span] = both.astype(jnp.bfloat16)
                to_partner(stage + 1, unit).start()

    def finish(unit):
        head, tile, span = where(unit)
        out_buf[...] = in_buf[head, span].astype(jnp.float32) + share[head, span].astype(jnp.float32)
        for stage in range(stages):
            @pl.when(above(stage))
            def _():
                out_buf[...] += recv[stage, head, span].astype(jnp.float32)
        out[0, span, columns(head)] = out_buf[...].astype(jnp.bfloat16)

    def step(count, carry):
        pl.when(count < units)(lambda: compute(count))
        for stage in range(stages):
            unit = count - (stage + 1) * LAG

            @pl.when((unit >= 0) & (unit < units))
            def _():
                combine(stage, unit)

        unit = count - stages * LAG

        @pl.when((unit >= 0) & (unit < units))
        def _():
            finish(unit)

        return carry

    lax.fori_loop(0, units + stages * LAG, step, 0)

    def drain(head, carry):
        @pl.when(has_right)
        def _():
            to_right(head).wait_send()

        @pl.when(has_left)
        def _():
            to_left(head).wait_send()

        return carry

    lax.fori_loop(0, heads, drain, 0)

    def drain_units(unit, carry):
        for stage in range(stages):
            @pl.when(sends(section, stage))
            def _():
                to_partner(stage, unit).wait_send()

        return carry

    lax.fori_loop(0, units, drain_units, 0)


def local(sections, tiles_axis, queries, keys_values, windows, gate_scales, stream_in):
    rows, width = queries.shape[1], queries.shape[2]
    heads = width // HEAD_DIM
    stages = sections.bit_length() - 1
    assert sections == 1 << stages
    half = (heads, rows, HEAD_DIM)
    units = heads * (rows // TILE)
    anywhere = pl.BlockSpec(memory_space=pl.ANY)
    dma = pltpu.SemaphoreType.DMA
    return pl.pallas_call(
        functools.partial(kernel, sections, tiles_axis),
        out_shape=jax.ShapeDtypeStruct((1, rows, width), jnp.bfloat16),
        in_specs=[
            pl.BlockSpec(memory_space=pltpu.SMEM),
            anywhere,
            anywhere,
            pl.BlockSpec(memory_space=pltpu.VMEM),
            anywhere,
        ],
        out_specs=pl.BlockSpec(memory_space=pltpu.VMEM),
        scratch_shapes=[
            pltpu.VMEM(half, jnp.bfloat16),
            pltpu.VMEM((heads, 2, rows, HEAD_DIM), jnp.bfloat16),
            pltpu.VMEM((heads, 2, HALO, HEAD_DIM), jnp.bfloat16),
            pltpu.VMEM((heads, 2, HALO, HEAD_DIM), jnp.bfloat16),
            pltpu.VMEM(half, jnp.bfloat16),
            pltpu.VMEM(half, jnp.bfloat16),
            pltpu.VMEM((max(stages, 1),) + half, jnp.bfloat16),
            pltpu.VMEM((max(stages - 1, 1),) + half, jnp.bfloat16),
            pltpu.VMEM((TILE, HEAD_DIM), jnp.float32),
            dma((heads,)),
            dma((heads,)),
            dma((heads,)),
            dma((2, heads)),
            dma((2, heads)),
            dma((max(stages, 1), units)),
            dma((max(stages, 1), units)),
        ],
        compiler_params=pltpu.CompilerParams(
            collective_id=0, has_side_effects=True, vmem_limit_bytes=VMEM_BYTES
        ),
    )(windows, queries, keys_values, gate_scales, stream_in)


def solution(mesh):
    placed = (
        P("section", "tile", None),
        P("section", None, "tile", None),
        P("tile", None),
        P("section", None),
        P("tile", None),
    )
    return jax.shard_map(
        functools.partial(local, mesh.shape["section"], mesh.shape["tile"]),
        mesh=mesh, in_specs=placed, out_specs=P("section", "tile", None), check_vma=False,
    )
```

time: 76.2 us -> 73.2 us (0.961)
  Pallas kernels: 72.5 us -> 70.1 us
    pallas_call x1, Pallas kernels: 72.5 us -> 70.1 us  [local(): pl.pallas_call(functools.partial(kernel, sections, tiles_axis), out_shape...]
    unnamed x1 -> x5, local copies, waits for them, and re-layouts: 3.4 us -> 2.87 us
where the time goes in v2:
time: 73.2 us; the launch traced here: 73 us
  Pallas kernels  70.1 us (96%)
  local copies, waits for them, and re-layouts  2.87 us (4%)
    pallas_call x1, Pallas kernels, local(): pl.pallas_call(functools.partial(kernel, sections, tiles_axis), out_shape...  70.1 us
    unnamed x5, local copies, waits for them, and re-layouts  2.87 us

profile of v2, /device:TPU:13, one launch (start us, length us, event | category | flops | bytes accessed | tf_op | source)
XLA Modules:
  0.0 73.0 jit_solution(16128952022321773990)
XLA Ops:
  0.0 0.0 copy-start
  0.0 0.7 copy-done
  0.7 0.0 copy-start.1
  0.7 0.7 copy-done.1
  1.4 70.1 %shard_map.55 = bf16[1,512,2560]{2,1,0:T(8,128)(2,1)S(1)} custom-call(s32[2,2]{1,0:T(2,128)S(1)} %copy-done.1, bf16[1,512,2560]{2,1,0:T(8,128)(2,1)} %queries.1, bf16[1,2,512,2560]{3,2,1,0:T(8,128)(2,1)} %keys_values.1, f32[1,2560]{1,0:T(1,128)S(1)} %copy-done, bf16[512,2560]{1,0:T(8,128)(2,1)} %stream_in.1), custom_call_target="tpu_custom_call" | custom-call | tf_op jit(solution)/shard_map/pallas_call | solution.py:303
  71.5 1.5 %copy.7 = bf16[1,512,2560]{2,1,0:T(8,128)(2,1)} copy(bf16[1,512,2560]{2,1,0:T(8,128)(2,1)S(1)} %shard_map.55) | data formatting | bytes 5242880
Async XLA Ops:
  0.0 0.7 copy-start
  0.7 0.7 copy-start.1

commit v3 on v2

--- a/solution.py
+++ b/solution.py
@@ -13,14 +13,15 @@
 REACH = 1
 HALO = REACH * TILE
 LAG = 3
-AHEAD = 3
+AHEAD = 2
 FAR = 1e30
 VMEM_BYTES = 50 * 1024 * 1024
 
 
 def kernel(
     sections, tiles_axis,
-    windows, queries, keys_values, gates, stream_in, out,
+    windows_in, queries, keys_values, gates_in, stream_in, out,
+    windows, gates, small_sem,
     q_buf, kv_buf, low, high, in_buf, share, recv, fwd, out_buf,
     q_sem, kv_sem, in_sem, halo_send, halo_recv, sec_send, sec_recv,
 ):
@@ -110,6 +111,10 @@
         def _():
             to_left(head).start()
 
+    small = (
+        pltpu.make_async_copy(windows_in, windows, small_sem.at[0]),
+        pltpu.make_async_copy(gates_in, gates, small_sem.at[1]),
+    )
     barrier = pltpu.get_barrier_semaphore()
 
     @pl.when(has_right)
@@ -130,23 +135,17 @@
             device_id_type=pl.DeviceIdType.MESH,
         )
     ahead = min(AHEAD, heads)
+    for copy in small:
+        copy.start()
     for head in range(ahead):
         load(head)
-
-    def clear(ref):
-        def one(head, carry):
-            ref[head] = jnp.zeros(ref.shape[1:], ref.dtype)
-            return carry
-
-        lax.fori_loop(0, heads, one, 0)
-
-    pl.when(jnp.logical_not(has_left))(lambda: clear(low))
-    pl.when(jnp.logical_not(has_right))(lambda: clear(high))
 
     pl.semaphore_wait(barrier, stages + has_left.astype(jnp.int32) + has_right.astype(jnp.int32))
     for head in range(ahead):
         send_halo(head)
 
+    for copy in small:
+        copy.wait()
     factor = math.log2(math.e) / math.sqrt(HEAD_DIM)
 
     def attend(head, tile):
@@ -205,6 +204,14 @@
             for copy in loads(head):
                 copy.wait()
 
+            @pl.when(jnp.logical_not(has_left))
+            def _():
+                low[head] = jnp.zeros(low.shape[1:], low.dtype)
+
+            @pl.when(jnp.logical_not(has_right))
+            def _():
+                high[head] = jnp.zeros(high.shape[1:], high.dtype)
+
         for at in range(local_tiles):
             @pl.when(tile == at)
             def _():
@@ -304,14 +311,17 @@
         functools.partial(kernel, sections, tiles_axis),
         out_shape=jax.ShapeDtypeStruct((1, rows, width), jnp.bfloat16),
         in_specs=[
-            pl.BlockSpec(memory_space=pltpu.SMEM),
-            anywhere,
-            anywhere,
-            pl.BlockSpec(memory_space=pltpu.VMEM),
+            anywhere,
+            anywhere,
+            anywhere,
+            anywhere,
             anywhere,
         ],
         out_specs=pl.BlockSpec(memory_space=pltpu.VMEM),
         scratch_shapes=[
+            pltpu.SMEM(windows.shape, windows.dtype),
+            pltpu.VMEM(gate_scales.shape, gate_scales.dtype),
+            dma((2,)),
             pltpu.VMEM(half, jnp.bfloat16),
             pltpu.VMEM((heads, 2, rows, HEAD_DIM), jnp.bfloat16),
             pltpu.VMEM((heads, 2, HALO, HEAD_DIM), jnp.bfloat16),

time: 73.2 us -> 72.6 us (level)
  no operation moved by 1% of the time
where the time goes in v3:
time: 72.6 us; the launch traced here: 72.4 us
  Pallas kernels  69.5 us (96%)
  local copies, waits for them, and re-layouts  2.87 us (4%)
    pallas_call x1, Pallas kernels, local(): pl.pallas_call(functools.partial(kernel, sections, tiles_axis), out_shape...  69.5 us
    unnamed x5, local copies, waits for them, and re-layouts  2.87 us

profile of v3, /device:TPU:13, one launch (start us, length us, event | category | flops | bytes accessed | tf_op | source)
XLA Modules:
  0.0 72.4 jit_solution(1743339675048146925)
XLA Ops:
  0.0 0.0 copy-start
  0.0 0.7 copy-done
  0.7 0.0 copy-start.1
  0.7 0.7 copy-done.1
  1.4 69.5 %shard_map.55 = bf16[1,512,2560]{2,1,0:T(8,128)(2,1)S(1)} custom-call(s32[2,2]{1,0:T(2,128)S(1)} %copy-done.1, bf16[1,512,2560]{2,1,0:T(8,128)(2,1)} %queries.1, bf16[1,2,512,2560]{3,2,1,0:T(8,128)(2,1)} %keys_values.1, f32[1,2560]{1,0:T(1,128)S(1)} %copy-done, bf16[512,2560]{1,0:T(8,128)(2,1)} %stream_in.1), custom_call_target="tpu_custom_call" | custom-call | tf_op jit(solution)/shard_map/pallas_call | solution.py:310
  70.9 1.5 %copy.7 = bf16[1,512,2560]{2,1,0:T(8,128)(2,1)} copy(bf16[1,512,2560]{2,1,0:T(8,128)(2,1)S(1)} %shard_map.55) | data formatting | bytes 5242880
Async XLA Ops:
  0.0 0.7 copy-start
  0.7 0.7 copy-start.1
